TPU v7x, 32 devices: a whole 2x2x4 slice. The times are simulated.
32 devices in a mesh: tile: 8 (over y, x, core), rep: 4 (over z).
Axes of the slice: x: 2, y: 2, z: 4, core: 2. Of those that a mesh axis runs over, the one named last changes fastest.
Arguments:
- features: bfloat16 [4, 32, 64, 512], P('rep', None, 'tile'), may hold values from -6 to 6
- cotangent: bfloat16 [4, 32, 64, 512], P('rep', None, 'tile'), may hold values from -6 to 6
- positions: int32 [4, 64], P('rep', 'tile'), may hold values from 0 to 16, as said below
- weight_first: bfloat16 [27, 32, 32], replicated, may hold values from -0.21875 to 0.21875
- weight_second: bfloat16 [27, 32, 32], replicated, may hold values from -0.21875 to 0.21875
- gain_first: float32 [32], replicated, may hold values from 0.4 to 1.6
- bias_first: float32 [32], replicated, may hold values from -3 to 3
- gain_second: float32 [32], replicated, may hold values from 0.4 to 1.6
- bias_second: float32 [32], replicated, may hold values from -3 to 3
Outputs:
- block_output: bfloat16 [4, 32, 64, 512], P('rep', None, 'tile')
- block_grad: bfloat16 [4, 32, 64, 512], P('rep', None, 'tile')
- grad_first: float32 [27, 32, 32], replicated
- grad_second: float32 [27, 32, 32], replicated
Inputs may be any that keep to these rules, and one draw needn't show every extreme that they name: In each region, a tile's 8 entries hold the positions of its active blocks in increasing order, then 16 in the entries left; every tile has at least one active block and some tile of every region has 8.
All inputs are finite; a program needn't handle non-finite values.
Results may differ from a plain program's by a relative error of at most 0.0057.
Values may be sent and summed in bfloat16 or wider, within the bound.
A program may use at most 128 MiB of HBM per device.

v0:
```python
import functools

import jax
import jax.numpy as jnp
from jax import lax
from jax.experimental import pallas as pl
from jax.experimental.pallas import tpu as pltpu
from jax.sharding import PartitionSpec as P

BS = 8
PX = 4
PY = 2
PZ = 2
TGY = 4
C = 32
X = PX * BS
Y = PY * BS
NPOS = PX * PY * PZ
NB = 8
HALO = 2
YS = Y + 2 * HALO
ROWS = (X + 2 * HALO) * YS
BASE = 16
TOTAL = BASE + ROWS + 16
WIDE_START, WIDE_ROWS = 8, 704
OWN_START, OWN_ROWS = HALO * YS, X * YS
EMPTY = 1024.0
GROUPS = 4
LANES = 128
F32 = jnp.float32
BF16 = jnp.bfloat16
MESH = pl.DeviceIdType.MESH
SHIFTS = [(t // 3 - 1) * YS + (t % 3 - 1) for t in range(9)]
WAYS = [(-1, 0), (1, 0), (0, -1), (0, 1), (-1, -1), (-1, 1), (1, -1), (1, 1)]


def first_cell(way, extent):
    return HALO if way < 0 else extent


def landing_cell(way, extent):
    return HALO + extent if way < 0 else 0


def kernel(
    tiles_x,
    slot_of,
    slot_pos,
    feats,
    cots,
    weights,
    scales,
    out_ref,
    grad_ref,
    wgrad_ref,
    raw,
    field,
    pre_one,
    hidden,
    cot,
    d_two,
    e_two,
    e_one,
    edge,
    taps_one,
    taps_two,
    taps_back,
    corner_taps,
    band,
    band_corner,
    turned,
    staged,
    send_x,
    send_y,
    send_c,
    recv_x,
    recv_y,
    recv_c,
    send_sem,
    recv_sem,
):
    me = lax.axis_index("tile")
    tx = me // TGY
    ty = me % TGY

    def exists(way, sign):
        ix, iy = tx + sign * way[0], ty + sign * way[1]
        return (ix >= 0) & (ix < tiles_x) & (iy >= 0) & (iy < TGY)

    def partner(way, sign):
        return me + sign * (way[0] * TGY + way[1])

    recv_x[0] = jnp.full(recv_x.shape[1:], EMPTY, BF16)
    recv_y[0] = jnp.full(recv_y.shape[1:], EMPTY, BF16)
    recv_c[0] = jnp.full(recv_c.shape[1:], EMPTY, BF16)
    recv_x[1] = jnp.zeros(recv_x.shape[1:], BF16)
    recv_y[1] = jnp.zeros(recv_y.shape[1:], BF16)
    recv_c[1] = jnp.zeros(recv_c.shape[1:], BF16)

    barrier = pltpu.get_barrier_semaphore()
    for way in WAYS:
        @pl.when(exists(way, 1))
        def _():
            pl.semaphore_signal(
                barrier, inc=1, device_id={"tile": partner(way, 1)}, device_id_type=MESH
            )

    def buffers(which, number):
        if number < 2:
            return send_x.at[which, number], recv_x.at[which, number]
        if number < 4:
            return send_y.at[which, number - 2], recv_y.at[which, number - 2]
        return send_c.at[which, number - 4], recv_c.at[which, number - 4]

    def transfer(which, number, sign):
        source, target = buffers(which, number)
        return pltpu.make_async_remote_copy(
            src_ref=source,
            dst_ref=target,
            send_sem=send_sem.at[which, number],
            recv_sem=recv_sem.at[which, number],
            device_id={"tile": partner(WAYS[number], sign)},
            device_id_type=MESH,
        )

    def pack(grid, which):
        for number, (wx, wy) in enumerate(WAYS):
            for g in range(GROUPS):
                lanes = slice(g * LANES, (g + 1) * LANES)
                if number < 2:
                    for k in range(HALO):
                        row = BASE + (first_cell(wx, X) + k) * YS + HALO
                        send_x[which, number, k * Y : (k + 1) * Y, lanes] = grid[
                            g, row : row + Y, :
                        ].astype(BF16)
                elif number < 4:
                    for k in range(HALO):
                        row = BASE + OWN_START + first_cell(wy, Y) + k
                        send_y[which, number - 2, k * X : (k + 1) * X, lanes] = grid[
                            g, pl.ds(row, X, stride=YS), :
                        ].astype(BF16)
                else:
                    row = BASE + first_cell(wx, X) * YS + first_cell(wy, Y)
                    both = [grid[g, row + k * YS : row + k * YS + 8, :] for k in range(HALO)]
                    send_c[which, number - 4, :, lanes] = jnp.concatenate(both, 0).astype(BF16)

    def start(which):
        for number, way in enumerate(WAYS):
            @pl.when(exists(way, 1))
            def _():
                transfer(which, number, 1).start()

    def finish(which):
        for number, way in enumerate(WAYS):
            @pl.when(exists(way, 1))
            def _():
                transfer(which, number, 1).wait_send()

            @pl.when(exists(way, -1))
            def _():
                transfer(which, number, -1).wait_recv()

    def unpack(grid, which):
        for number, (wx, wy) in enumerate(WAYS):
            for g in range(GROUPS):
                lanes = slice(g * LANES, (g + 1) * LANES)
                if number < 2:
                    for k in range(HALO):
                        row = BASE + (landing_cell(wx, X) + k) * YS + HALO
                        grid[g, row : row + Y, :] = recv_x[
                            which, number, k * Y : (k + 1) * Y, lanes
                        ].astype(F32)
                elif number < 4:
                    for k in range(HALO):
                        row = BASE + OWN_START + landing_cell(wy, Y) + k
                        grid[g, pl.ds(row, X, stride=YS), :] = recv_y[
                            which, number - 2, k * X : (k + 1) * X, lanes
                        ].astype(F32)
                else:
                    both = recv_c[which, number - 4, :, lanes].astype(F32)
                    for k in range(HALO):
                        row = BASE + (landing_cell(wx, X) + k) * YS + landing_cell(wy, Y)
                        grid[g, row : row + HALO, :] = both[k * 8 : k * 8 + HALO]

    def block_rows(p, i):
        px, py = p // (PY * PZ), p // PZ % PY
        return BASE + (HALO + px * BS + i) * YS + HALO + py * BS

    def spread(blocks, grid):
        for p in range(NPOS):
            block = blocks[slot_of[p]].astype(F32)
            for i in range(BS):
                row = block_rows(p, i)
                for half in range(2):
                    grid[p % PZ * 2 + half, row : row + BS, :] = block[
                        i * BS : (i + 1) * BS, half * LANES : (half + 1) * LANES
                    ]

    def collect(grid, result):
        staged[NPOS] = jnp.zeros(staged.shape[1:], BF16)
        for p in range(NPOS):
            for half in range(2):
                pieces = [
                    grid[p % PZ * 2 + half, block_rows(p, i) : block_rows(p, i) + BS, :]
                    for i in range(BS)
                ]
                staged[p, :, half * LANES : (half + 1) * LANES] = jnp.concatenate(
                    pieces, 0
                ).astype(BF16)
        for s in range(NB):
            result[s] = staged[slot_pos[s]]

    for g in range(GROUPS):
        raw[g] = jnp.full((TOTAL, LANES), EMPTY, F32)
        cot[g] = jnp.zeros((TOTAL, LANES), F32)
        e_two[g] = jnp.zeros((TOTAL, LANES), F32)
    spread(feats, raw)
    pack(raw, 0)
    pl.semaphore_wait(barrier, sum(exists(way, 1).astype(jnp.int32) for way in WAYS))
    start(0)

    lane_group = lax.broadcasted_iota(jnp.int32, (C, LANES), 1) // C
    picks = [(lane_group == k).astype(F32).astype(BF16) for k in range(4)]
    for w in range(4):
        band_corner[w] = jnp.zeros(band_corner.shape[1:], BF16)

    def build(step, carry):
        w = step // 9
        t = step % 9
        three = [weights[w, t * 3 + k] for k in range(3)]
        row = pl.multiple_of(t * 256, 256)
        for z_in in range(8):
            for tile in range(2):
                total = None
                for k in range(4):
                    dz = z_in - (tile * 4 + k)
                    if abs(dz) <= 1:
                        term = three[dz + 1] * picks[k]
                        total = term if total is None else total + term
                if total is None:
                    total = jnp.zeros((C, LANES), BF16)
                band[w, pl.ds(row + z_in * C, C), tile * LANES : (tile + 1) * LANES] = total
        edge_row = pl.multiple_of(t * 64, 64)
        band_corner[w, pl.ds(edge_row, C), LANES:] = three[0] * picks[0]
        band_corner[w, pl.ds(edge_row + C, C), :LANES] = three[2] * picks[3]
        return carry

    lax.fori_loop(0, 36, build, 0)
    spread(cots, cot)

    def gather_taps(grid, taps, first, rows):
        lane = lax.broadcasted_iota(jnp.int32, (TOTAL, LANES), 1)
        pair = jnp.where(
            lane < C,
            pltpu.roll(grid[1], C, 1),
            jnp.where(lane < 2 * C, pltpu.roll(grid[2], C, 1), 0.0),
        )
        edge[0] = pair
        edge[1] = pltpu.roll(pair, 2 * C, 1)
        for t in range(9):
            begin = BASE + first + SHIFTS[t]
            for g in range(GROUPS):
                lanes = slice(t * 256 + g % 2 * LANES, t * 256 + g % 2 * LANES + LANES)
                taps[g // 2, :rows, lanes] = grid[g, begin : begin + rows, :].astype(BF16)
        for j in range(5):
            begin = BASE + first + SHIFTS[2 * j]
            value = edge[0, begin : begin + rows, :]
            if j < 4:
                begin = BASE + first + SHIFTS[2 * j + 1]
                value = value + edge[1, begin : begin + rows, :]
            corner_taps[:rows, j * LANES : (j + 1) * LANES] = value.astype(BF16)

    def convolve(taps, w, first, rows, finish_group):
        chunk = rows // 2

        def step(c, carry):
            here = pl.ds(pl.multiple_of(c * chunk, 16), chunk)
            low = jnp.dot(taps[0, here, :], band[w], preferred_element_type=F32)
            high = jnp.dot(taps[1, here, :], band[w], preferred_element_type=F32)
            mid = jnp.dot(corner_taps[here, :], band_corner[w], preferred_element_type=F32)
            there = pl.ds(pl.multiple_of(BASE + first + c * chunk, 8), chunk)
            finish_group(0, there, low[:, :LANES])
            finish_group(1, there, low[:, LANES:] + mid[:, :LANES])
            finish_group(2, there, high[:, :LANES] + mid[:, LANES:])
            finish_group(3, there, high[:, LANES:])
            return carry

        lax.fori_loop(0, 2, step, 0)

    def weight_gradient(taps, offset, which):
        for half in range(2):
            left = slice(half * 224, half * 224 + 288)

            def step(t, carry):
                lanes = pl.ds(pl.multiple_of(t * 256, 256), 256)
                product = jnp.dot(
                    turned[left, :],
                    taps[half, offset : offset + OWN_ROWS, lanes],
                    preferred_element_type=F32,
                )
                for dz in range(-1, 2):
                    total = jnp.zeros((C, LANES), F32)
                    for b in range(8):
                        a = b + half - dz
                        if 0 <= a <= 8:
                            part = product[
                                a * C : (a + 1) * C, b // 4 * LANES : (b // 4 + 1) * LANES
                            ]
                            total = total + jnp.where(lane_group == b % 4, part, 0.0)
                    total = total + pltpu.roll(total, 64, 1)
                    total = total + pltpu.roll(total, 32, 1)
                    if half == 0:
                        wgrad_ref[which, t * 3 + dz + 1] = total
                    else:
                        wgrad_ref[which, t * 3 + dz + 1] += total
                return carry

            lax.fori_loop(0, 9, step, 0)

    gain_one, bias_one = scales[0:1, :], scales[1:2, :]
    gain_two, bias_two = scales[2:3, :], scales[3:4, :]

    finish(0)
    unpack(raw, 0)
    for g in range(GROUPS):
        value = raw[g]
        field[g] = jnp.where(value < 512.0, value, 0.0)

    gather_taps(field, taps_one, WIDE_START, WIDE_ROWS)

    def after_first(g, rows, value):
        pre = value * gain_one + bias_one
        pre_one[g, rows, :] = pre
        act = pre / (1.0 + jnp.exp(-pre))
        act = jnp.where(raw[g, rows, :] < 512.0, act, 0.0)
        hidden[g, rows, :] = act.astype(BF16).astype(F32)

    convolve(taps_one, 0, WIDE_START, WIDE_ROWS, after_first)

    gather_taps(hidden, taps_two, OWN_START, OWN_ROWS)

    def after_second(g, rows, value):
        pre = value * gain_two + bias_two + field[g, rows, :]
        s = 1.0 / (1.0 + jnp.exp(-pre))
        hidden[g, rows, :] = pre * s
        d = cot[g, rows, :] * (s + pre * s * (1.0 - s))
        d_two[g, rows, :] = d
        e_two[g, rows, :] = (d * gain_two).astype(BF16).astype(F32)

    convolve(taps_two, 1, OWN_START, OWN_ROWS, after_second)

    pack(e_two, 1)
    start(1)
    own = slice(BASE + OWN_START, BASE + OWN_START + OWN_ROWS)
    for g in range(GROUPS):
        turned[g * LANES : (g + 1) * LANES, :] = jnp.transpose(e_two[g, own, :]).astype(BF16)
    weight_gradient(taps_two, 0, 1)
    collect(hidden, out_ref)
    finish(1)
    unpack(e_two, 1)

    gather_taps(e_two, taps_back, WIDE_START, WIDE_ROWS)

    def after_third(g, rows, value):
        pre = pre_one[g, rows, :]
        s = 1.0 / (1.0 + jnp.exp(-pre))
        e = value * (s + pre * s * (1.0 - s)) * gain_one
        e = jnp.where(raw[g, rows, :] < 512.0, e, 0.0)
        e_one[g, rows, :] = e.astype(BF16).astype(F32)

    convolve(taps_back, 2, WIDE_START, WIDE_ROWS, after_third)

    gather_taps(e_one, taps_back, OWN_START, OWN_ROWS)

    def after_fourth(g, rows, value):
        d_two[g, rows, :] = d_two[g, rows, :] + value

    convolve(taps_back, 3, OWN_START, OWN_ROWS, after_fourth)
    collect(d_two, grad_ref)
    y_cell = lax.rem(lax.broadcasted_iota(jnp.int32, (OWN_ROWS, LANES), 0), YS)
    inside = (y_cell >= HALO) & (y_cell < HALO + Y)
    for g in range(GROUPS):
        turned[g * LANES : (g + 1) * LANES, :] = jnp.transpose(
            jnp.where(inside, e_one[g, own, :], 0.0)
        ).astype(BF16)
    weight_gradient(taps_one, OWN_START - WIDE_START, 0)


def per_device(
    tiles_x,
    voxels,
    features,
    cotangent,
    positions,
    weight_first,
    weight_second,
    gain_first,
    bias_first,
    gain_second,
    bias_second,
):
    slot_pos = positions[0]
    matches = jnp.arange(NPOS, dtype=jnp.int32)[:, None] == slot_pos[None, :]
    slot_index = jnp.sum(jnp.where(matches, jnp.arange(NB, dtype=jnp.int32)[None, :], 0), axis=1)
    slot_of = jnp.where(jnp.any(matches, axis=1), slot_index, NB).astype(jnp.int32)

    def to_rows(compact, empty):
        blocks = compact[0].reshape(C, NB, BS * BS, BS).transpose(1, 2, 3, 0)
        blocks = blocks.reshape(NB, BS * BS, BS * C)
        return jnp.concatenate([blocks, jnp.full((1, BS * BS, BS * C), empty, BF16)], axis=0)

    def from_rows(blocks):
        result = blocks.reshape(NB, BS * BS, BS, C).transpose(3, 0, 1, 2)
        return result.reshape(1, C, NB, BS**3)

    def forward(weight):
        return jnp.tile(weight.transpose(0, 2, 1), (1, 1, 4))

    def backward(weight):
        return jnp.tile(weight[::-1], (1, 1, 4))

    weights = jnp.stack(
        [
            forward(weight_first),
            forward(weight_second),
            backward(weight_second),
            backward(weight_first),
        ]
    )
    scales = jnp.tile(jnp.stack([gain_first, bias_first, gain_second, bias_second]), (1, 4))
    grid = pltpu.VMEM((GROUPS, TOTAL, LANES), F32)
    smem = pl.BlockSpec(memory_space=pltpu.SMEM)
    vmem = pl.BlockSpec(memory_space=pltpu.VMEM)
    block_output, block_grad, wgrad = pl.pallas_call(
        functools.partial(kernel, tiles_x),
        out_shape=(
            jax.ShapeDtypeStruct((NB, BS * BS, BS * C), BF16),
            jax.ShapeDtypeStruct((NB, BS * BS, BS * C), BF16),
            jax.ShapeDtypeStruct((2, 27, C, LANES), F32),
        ),
        in_specs=[smem, smem, vmem, vmem, vmem, vmem],
        out_specs=(vmem, vmem, vmem),
        scratch_shapes=[
            grid,
            grid,
            grid,
            grid,
            grid,
            grid,
            grid,
            grid,
            pltpu.VMEM((2, TOTAL, LANES), F32),
            pltpu.VMEM((2, WIDE_ROWS, 9 * 256), BF16),
            pltpu.VMEM((2, OWN_ROWS, 9 * 256), BF16),
            pltpu.VMEM((2, WIDE_ROWS, 9 * 256), BF16),
            pltpu.VMEM((WIDE_ROWS, 5 * LANES), BF16),
            pltpu.VMEM((4, 9 * 256, 256), BF16),
            pltpu.VMEM((4, 5 * LANES, 256), BF16),
            pltpu.VMEM((GROUPS * LANES, OWN_ROWS), BF16),
            pltpu.VMEM((NPOS + 1, BS * BS, BS * C), BF16),
            pltpu.VMEM((2, 2, HALO * Y, 512), BF16),
            pltpu.VMEM((2, 2, HALO * X, 512), BF16),
            pltpu.VMEM((2, 4, 16, 512), BF16),
            pltpu.VMEM((2, 2, HALO * Y, 512), BF16),
            pltpu.VMEM((2, 2, HALO * X, 512), BF16),
            pltpu.VMEM((2, 4, 16, 512), BF16),
            pltpu.SemaphoreType.DMA((2, 8)),
            pltpu.SemaphoreType.DMA((2, 8)),
        ],
        compiler_params=pltpu.CompilerParams(
            collective_id=0, has_side_effects=True, vmem_limit_bytes=60 * 1024 * 1024
        ),
    )(slot_of, slot_pos, to_rows(features, EMPTY), to_rows(cotangent, 0.0), weights, scales)
    local = wgrad[:, :, :, :C] * (1.0 / jnp.sqrt(jnp.float32(voxels)))
    summed = lax.psum(local, ("tile", "rep"))
    return from_rows(block_output), from_rows(block_grad), summed[0], summed[1]


def solution(mesh):
    split = P("rep", None, "tile", None)
    tiles, regions = mesh.shape["tile"], mesh.shape["rep"]
    return jax.shard_map(
        functools.partial(per_device, tiles // TGY, tiles * regions * NB * BS**3),
        mesh=mesh,
        in_specs=(split, split, P("rep", "tile"), P(), P(), P(), P(), P(), P()),
        out_specs=(split, split, P(), P()),
        check_vma=False,
    )
```

profile of v0, /device:TPU:0, one launch (start us, length us, event | category | flops | bytes accessed | tf_op | source)
XLA Modules:
  0.0 203.3 jit_solution(18030903920637818794)
XLA Ops:
  7.2 0.6 copy-done.6
  8.0 0.6 copy-done.10
  8.7 0.7 tile.50.scales
  9.4 1.0 rev.6
  10.6 0.8 copy-done.1
  14.9 0.5 copy-done.2
  15.4 0.5 copy.33
  15.9 0.6 copy.34
  16.8 0.7 copy-done.3
  17.5 0.5 copy.36
  18.0 0.6 copy.37
  18.9 0.5 broadcast_select_fusion.slot_of
  19.4 0.7 concatenate.6.feats
  20.1 0.7 concatenate.7.cots
  20.9 1.0 pad_maximum_fusion.weights
  21.9 40.0 %shard_map.120 = (bf16[8,64,256]{2,1,0:T(8,128)(2,1)}, bf16[8,64,256]{2,1,0:T(8,128)(2,1)}, f32[2,27,32,128]{3,2,1,0:T(8,128)}) custom-call(s32[16]{0:T(128)} %broadcast_select_fusion.slot_of, s32[8]{0:T(128)} %bitcast.37, bf16[9,64,256]{2,1,0:T(8,128)(2,1)} %concatenate.6.feats, bf16[9,64,256]{2,1,0:T(8,128)(2,1)} %concatenate.7.cots, ...), custom_call_target="tpu_custom_call" | custom-call | tf_op jit(solution)/shard_map/pallas_call | solution.py:434
  61.9 2.2 %slice_multiply_fusion = f32[2,27,32,32]{3,2,1,0:T(8,128)} fusion(f32[2,27,32,128]{3,2,1,0:T(8,128)} %get-tuple-element.9), kind=kLoop, calls=%fused_computation.1 | loop fusion | flops 55296 | bytes 442368 | tf_op jit(solution)/shard_map/mul | solution.py:474
  64.1 0.9 copy-done.5
  65.3 0.6 copy.42
  65.9 1.2 copy.45
  67.4 0.6 copy.44
  68.0 1.2 copy.46
  69.2 125.2 %all-reduce.4.cloned.1.call-done = f32[2,27,32,32]{3,2,1,0:T(8,128)} async-done(((f32[2,27,32,32]{3,2,1,0:T(8,128)}), f32[2,27,32,32]{3,2,1,0:T(8,128)}) %all-reduce.4.cloned.1.call-update) | async-done | bytes 221200 | tf_op jit(solution)/shard_map/psum | solution.py:475
  194.4 2.1 %slice_bitcast_fusion = (f32[27,32,32]{2,1,0:T(8,128)}, f32[27,32,32]{2,1,0:T(8,128)}) fusion(f32[2,27,32,32]{3,2,1,0:T(8,128)} %all-reduce.4.cloned.1.call-done), kind=kLoop, calls=%fused_computation.2 | loop fusion | bytes 442368 | tf_op jit(solution)/shard_map/squeeze | solution.py:476
  (37 shorter events, 4.9 us)
Async XLA Ops:
  7.2 0.7 copy-start.6
  7.2 187.2 %all-reduce.4.cloned.1.call-start = ((), (), s32[]{:S(2)}) async-start(), calls=%async_computation | async-start | bytes 1769472 | tf_op jit(solution)/shard_map/psum | solution.py:475
  8.0 0.7 copy-start.10
  8.0 0.7 copy-start.7
  8.0 0.7 copy-start.8
  8.0 0.7 copy-start.9
  9.4 1.0 copy-start
  10.4 0.9 copy-start.1
  14.4 1.0 copy-start.2
  16.6 1.0 copy-start.3
  64.1 0.9 copy-start.5
  65.9 1.3 copy-start.4
Sparse Core Ops, SparseCore 0:
  64.2 130.1 all-reduce.3
where the time goes:
time: 204 us; the launch traced here: 203 us
  waiting for transfers between devices  125 us (61%)
  Pallas kernels  40 us (20%)
  local copies, waits for them, and re-layouts  20 us (10%)
  between operations  14.2 us (7%)
  other arithmetic  3.94 us (2%)
    psum x1, waiting for transfers between devices, per_device(): summed = lax.psum(local, ('tile', 'rep'))  125 us
    pallas_call x1, Pallas kernels, per_device(): pl.pallas_call(functools.partial(kernel, tiles_x), out_shape=(jax.ShapeDt...  40 us
    unnamed x26, local copies, waits for them, and re-layouts  7.76 us
  transfers between devices with their start and end apart: 1, of which 1 were waited for; matrix products, arithmetic and copies ran while one was open for 2% of the time, Pallas kernels for 0%

commit v1 on v0

--- a/solution.py
+++ b/solution.py
@@ -25,6 +25,7 @@
 WIDE_START, WIDE_ROWS = 8, 704
 OWN_START, OWN_ROWS = HALO * YS, X * YS
 EMPTY = 1024.0
+SUM_ROWS = 256
 GROUPS = 4
 LANES = 128
 F32 = jnp.float32
@@ -43,16 +44,22 @@
 
 
 def kernel(
-    tiles_x,
-    slot_of,
-    slot_pos,
+    tiles,
+    regions,
+    scale,
+    positions,
     feats,
     cots,
-    weights,
-    scales,
+    weight_first,
+    weight_second,
+    gain_first,
+    bias_first,
+    gain_second,
+    bias_second,
     out_ref,
     grad_ref,
-    wgrad_ref,
+    wgrad_first,
+    wgrad_second,
     raw,
     field,
     pre_one,
@@ -76,10 +83,26 @@
     recv_x,
     recv_y,
     recv_c,
+    flat,
+    spun,
+    blocks,
+    sums,
+    scattered,
+    parts,
+    totals,
     send_sem,
     recv_sem,
+    scatter_send,
+    scatter_recv,
+    part_send,
+    part_recv,
+    total_send,
+    total_recv,
 ):
     me = lax.axis_index("tile")
+    rep_me = lax.axis_index("rep")
+    tiles_x = tiles // TGY
+    piece = SUM_ROWS // tiles
     tx = me // TGY
     ty = me % TGY
 
@@ -98,12 +121,14 @@
     recv_c[1] = jnp.zeros(recv_c.shape[1:], BF16)
 
     barrier = pltpu.get_barrier_semaphore()
-    for way in WAYS:
-        @pl.when(exists(way, 1))
-        def _():
-            pl.semaphore_signal(
-                barrier, inc=1, device_id={"tile": partner(way, 1)}, device_id_type=MESH
-            )
+    for k in range(1, tiles):
+        pl.semaphore_signal(
+            barrier, inc=1, device_id={"tile": lax.rem(me + k, tiles)}, device_id_type=MESH
+        )
+    for k in range(1, regions):
+        pl.semaphore_signal(
+            barrier, inc=1, device_id={"rep": lax.rem(rep_me + k, regions)}, device_id_type=MESH
+        )
 
     def buffers(which, number):
         if number < 2:
@@ -186,9 +211,39 @@
         px, py = p // (PY * PZ), p // PZ % PY
         return BASE + (HALO + px * BS + i) * YS + HALO + py * BS
 
-    def spread(blocks, grid):
+    lane_group = lax.broadcasted_iota(jnp.int32, (C, LANES), 1) // C
+    tall_group = lax.broadcasted_iota(jnp.int32, (BS * BS, LANES), 1) // C
+    copies = (
+        lax.broadcasted_iota(jnp.int32, (C, LANES), 1) % C
+        == lax.broadcasted_iota(jnp.int32, (C, LANES), 0)
+    ).astype(F32).astype(BF16)
+
+    def slot_at(p):
+        slot = NB
+        for s in range(NB):
+            slot = jnp.where(positions[0, s] == p, s, slot)
+        return slot
+
+    slots = [slot_at(p) for p in range(NPOS)]
+
+    def spread(source, grid, empty):
+        for g in range(GROUPS):
+            flat[g] = source[:, g * LANES : (g + 1) * LANES].astype(F32)
+        for s in range(NB):
+            for g in range(GROUPS):
+                part = flat[g, pl.ds(s, C, stride=NB), :].astype(BF16)
+                spun[s, g * LANES : (g + 1) * LANES, :] = lax.dot_general(
+                    part, copies, (((0,), (0,)), ((), ())), preferred_element_type=F32
+                )
+            for half in range(2):
+                total = spun[s, pl.ds(half * 4, BS * BS, stride=BS), :]
+                for k in range(1, 4):
+                    other = spun[s, pl.ds(half * 4 + k, BS * BS, stride=BS), :]
+                    total = jnp.where(tall_group == k, other, total)
+                blocks[s, :, half * LANES : (half + 1) * LANES] = total
+        blocks[NB] = jnp.full(blocks.shape[1:], empty, F32)
         for p in range(NPOS):
-            block = blocks[slot_of[p]].astype(F32)
+            block = blocks[slots[p]]
             for i in range(BS):
                 row = block_rows(p, i)
                 for half in range(2):
@@ -197,37 +252,120 @@
                     ]
 
     def collect(grid, result):
-        staged[NPOS] = jnp.zeros(staged.shape[1:], BF16)
+        staged[NPOS] = jnp.zeros(staged.shape[1:], F32)
         for p in range(NPOS):
             for half in range(2):
-                pieces = [
-                    grid[p % PZ * 2 + half, block_rows(p, i) : block_rows(p, i) + BS, :]
-                    for i in range(BS)
-                ]
-                staged[p, :, half * LANES : (half + 1) * LANES] = jnp.concatenate(
-                    pieces, 0
-                ).astype(BF16)
+                for i in range(BS):
+                    row = block_rows(p, i)
+                    staged[p, i * BS : (i + 1) * BS, half * LANES : (half + 1) * LANES] = grid[
+                        p % PZ * 2 + half, row : row + BS, :
+                    ]
         for s in range(NB):
-            result[s] = staged[slot_pos[s]]
+            block = staged[positions[0, s]]
+            for k in range(BS):
+                part = block[:, k // 4 * LANES : (k // 4 + 1) * LANES]
+                spun[s, pl.ds(k, BS * BS, stride=BS), :] = jnp.where(
+                    tall_group == k % 4, part, 0.0
+                )
+            for g in range(GROUPS):
+                flat[g, pl.ds(s, C, stride=NB), :] = lax.dot_general(
+                    copies,
+                    spun[s, g * LANES : (g + 1) * LANES, :].astype(BF16),
+                    (((1,), (1,)), ((), ())),
+                    preferred_element_type=F32,
+                )
+        for g in range(GROUPS):
+            result[:, g * LANES : (g + 1) * LANES] = flat[g].astype(BF16)
+
+    def scatter_copy(w, k):
+        peer = lax.rem(me + k, tiles)
+        return pltpu.make_async_remote_copy(
+            src_ref=sums.at[w, pl.ds(pl.multiple_of(peer * piece, 8), piece), :],
+            dst_ref=scattered.at[w, k],
+            send_sem=scatter_send.at[w, k],
+            recv_sem=scatter_recv.at[w, k],
+            device_id={"tile": peer},
+            device_id_type=MESH,
+        )
+
+    def part_copy(w, k):
+        return pltpu.make_async_remote_copy(
+            src_ref=parts.at[w, rep_me],
+            dst_ref=parts.at[w, rep_me],
+            send_sem=part_send.at[w, k],
+            recv_sem=part_recv.at[w, k],
+            device_id={"rep": lax.rem(rep_me + k, regions)},
+            device_id_type=MESH,
+        )
+
+    own_piece = pl.ds(pl.multiple_of(me * piece, 8), piece)
+
+    def total_copy(w, k):
+        return pltpu.make_async_remote_copy(
+            src_ref=totals.at[w, own_piece, :],
+            dst_ref=totals.at[w, own_piece, :],
+            send_sem=total_send.at[w, k],
+            recv_sem=total_recv.at[w, k],
+            device_id={"tile": lax.rem(me + k, tiles)},
+            device_id_type=MESH,
+        )
+
+    def scatter_start(w):
+        for k in range(1, tiles):
+            scatter_copy(w, k).start()
+
+    def scatter_finish(w):
+        total = sums[w, own_piece, :]
+        for k in range(1, tiles):
+            scatter_copy(w, k).wait()
+            total = total + scattered[w, k]
+        parts[w, rep_me] = total * scale
+        for k in range(1, regions):
+            part_copy(w, k).start()
+
+    def part_finish(w):
+        for k in range(1, regions):
+            part_copy(w, k).wait()
+        total = parts[w, 0]
+        for r in range(1, regions):
+            total = total + parts[w, r]
+        totals[w, own_piece, :] = total
+        for k in range(1, tiles):
+            total_copy(w, k).start()
+
+    def total_finish(w, result):
+        for k in range(1, tiles):
+            total_copy(w, k).wait()
+        for q in range(27):
+            block = totals[w, q // 4 * C : (q // 4 + 1) * C, :]
+            if q % 4:
+                block = pltpu.roll(block, LANES - q % 4 * C, 1)
+            result[q] = block[:, :C]
 
     for g in range(GROUPS):
         raw[g] = jnp.full((TOTAL, LANES), EMPTY, F32)
         cot[g] = jnp.zeros((TOTAL, LANES), F32)
         e_two[g] = jnp.zeros((TOTAL, LANES), F32)
-    spread(feats, raw)
+    spread(feats, raw, EMPTY)
     pack(raw, 0)
-    pl.semaphore_wait(barrier, sum(exists(way, 1).astype(jnp.int32) for way in WAYS))
+    pl.semaphore_wait(barrier, tiles + regions - 2)
     start(0)
 
-    lane_group = lax.broadcasted_iota(jnp.int32, (C, LANES), 1) // C
     picks = [(lane_group == k).astype(F32).astype(BF16) for k in range(4)]
     for w in range(4):
         band_corner[w] = jnp.zeros(band_corner.shape[1:], BF16)
 
-    def build(step, carry):
-        w = step // 9
-        t = step % 9
-        three = [weights[w, t * 3 + k] for k in range(3)]
+    def turned_weight(ref, q):
+        block = lax.dot_general(
+            ref[q], copies, (((0,), (0,)), ((), ())), preferred_element_type=F32
+        )
+        return block.astype(BF16)
+
+    def plain_weight(ref, q):
+        return jnp.dot(ref[26 - q], copies, preferred_element_type=F32).astype(BF16)
+
+    def build_one(w, ref, read, t):
+        three = [read(ref, t * 3 + k) for k in range(3)]
         row = pl.multiple_of(t * 256, 256)
         for z_in in range(8):
             for tile in range(2):
@@ -243,10 +381,16 @@
         edge_row = pl.multiple_of(t * 64, 64)
         band_corner[w, pl.ds(edge_row, C), LANES:] = three[0] * picks[0]
         band_corner[w, pl.ds(edge_row + C, C), :LANES] = three[2] * picks[3]
+
+    def build(t, carry):
+        build_one(0, weight_first, turned_weight, t)
+        build_one(1, weight_second, turned_weight, t)
+        build_one(2, weight_second, plain_weight, t)
+        build_one(3, weight_first, plain_weight, t)
         return carry
 
-    lax.fori_loop(0, 36, build, 0)
-    spread(cots, cot)
+    lax.fori_loop(0, 9, build, 0)
+    spread(cots, cot, 0.0)
 
     def gather_taps(grid, taps, first, rows):
         lane = lax.broadcasted_iota(jnp.int32, (TOTAL, LANES), 1)
@@ -288,37 +432,41 @@
         lax.fori_loop(0, 2, step, 0)
 
     def weight_gradient(taps, offset, which):
-        for half in range(2):
-            left = slice(half * 224, half * 224 + 288)
-
-            def step(t, carry):
-                lanes = pl.ds(pl.multiple_of(t * 256, 256), 256)
-                product = jnp.dot(
-                    turned[left, :],
+        def step(t, carry):
+            lanes = pl.ds(pl.multiple_of(t * 256, 256), 256)
+            products = [
+                jnp.dot(
+                    turned[half * 224 : half * 224 + 288, :],
                     taps[half, offset : offset + OWN_ROWS, lanes],
                     preferred_element_type=F32,
                 )
-                for dz in range(-1, 2):
-                    total = jnp.zeros((C, LANES), F32)
+                for half in range(2)
+            ]
+            for dz in range(-1, 2):
+                total = jnp.zeros((C, LANES), F32)
+                for half in range(2):
                     for b in range(8):
                         a = b + half - dz
                         if 0 <= a <= 8:
-                            part = product[
+                            part = products[half][
                                 a * C : (a + 1) * C, b // 4 * LANES : (b // 4 + 1) * LANES
                             ]
                             total = total + jnp.where(lane_group == b % 4, part, 0.0)
-                    total = total + pltpu.roll(total, 64, 1)
-                    total = total + pltpu.roll(total, 32, 1)
-                    if half == 0:
-                        wgrad_ref[which, t * 3 + dz + 1] = total
-                    else:
-                        wgrad_ref[which, t * 3 + dz + 1] += total
-                return carry
-
-            lax.fori_loop(0, 9, step, 0)
-
-    gain_one, bias_one = scales[0:1, :], scales[1:2, :]
-    gain_two, bias_two = scales[2:3, :], scales[3:4, :]
+                total = total + pltpu.roll(total, 64, 1)
+                total = total + pltpu.roll(total, 32, 1)
+                q = t * 3 + (dz + 1)
+                rows = pl.ds(pl.multiple_of(lax.div(q, 4) * C, C), C)
+                sums[which, rows, :] += jnp.where(lane_group == lax.rem(q, 4), total, 0.0)
+            return carry
+
+        lax.fori_loop(0, 9, step, 0)
+
+    def wide(ref):
+        return jnp.concatenate([ref[...]] * 4, axis=1)
+
+    sums[...] = jnp.zeros(sums.shape, F32)
+    gain_one, bias_one = wide(gain_first), wide(bias_first)
+    gain_two, bias_two = wide(gain_second), wide(bias_second)
 
     finish(0)
     unpack(raw, 0)
@@ -355,6 +503,7 @@
     for g in range(GROUPS):
         turned[g * LANES : (g + 1) * LANES, :] = jnp.transpose(e_two[g, own, :]).astype(BF16)
     weight_gradient(taps_two, 0, 1)
+    scatter_start(1)
     collect(hidden, out_ref)
     finish(1)
     unpack(e_two, 1)
@@ -370,13 +519,7 @@
 
     convolve(taps_back, 2, WIDE_START, WIDE_ROWS, after_third)
 
-    gather_taps(e_one, taps_back, OWN_START, OWN_ROWS)
-
-    def after_fourth(g, rows, value):
-        d_two[g, rows, :] = d_two[g, rows, :] + value
-
-    convolve(taps_back, 3, OWN_START, OWN_ROWS, after_fourth)
-    collect(d_two, grad_ref)
+    scatter_finish(1)
     y_cell = lax.rem(lax.broadcasted_iota(jnp.int32, (OWN_ROWS, LANES), 0), YS)
     inside = (y_cell >= HALO) & (y_cell < HALO + Y)
     for g in range(GROUPS):
@@ -384,11 +527,25 @@
             jnp.where(inside, e_one[g, own, :], 0.0)
         ).astype(BF16)
     weight_gradient(taps_one, OWN_START - WIDE_START, 0)
+    scatter_start(0)
+    part_finish(1)
+
+    gather_taps(e_one, taps_back, OWN_START, OWN_ROWS)
+    scatter_finish(0)
+
+    def after_fourth(g, rows, value):
+        d_two[g, rows, :] = d_two[g, rows, :] + value
+
+    convolve(taps_back, 3, OWN_START, OWN_ROWS, after_fourth)
+    part_finish(0)
+    collect(d_two, grad_ref)
+    total_finish(1, wgrad_second)
+    total_finish(0, wgrad_first)
 
 
 def per_device(
-    tiles_x,
-    voxels,
+    tiles,
+    regions,
     features,
     cotangent,
     positions,
@@ -399,47 +556,27 @@
     gain_second,
     bias_second,
 ):
-    slot_pos = positions[0]
-    matches = jnp.arange(NPOS, dtype=jnp.int32)[:, None] == slot_pos[None, :]
-    slot_index = jnp.sum(jnp.where(matches, jnp.arange(NB, dtype=jnp.int32)[None, :], 0), axis=1)
-    slot_of = jnp.where(jnp.any(matches, axis=1), slot_index, NB).astype(jnp.int32)
-
-    def to_rows(compact, empty):
-        blocks = compact[0].reshape(C, NB, BS * BS, BS).transpose(1, 2, 3, 0)
-        blocks = blocks.reshape(NB, BS * BS, BS * C)
-        return jnp.concatenate([blocks, jnp.full((1, BS * BS, BS * C), empty, BF16)], axis=0)
-
-    def from_rows(blocks):
-        result = blocks.reshape(NB, BS * BS, BS, C).transpose(3, 0, 1, 2)
-        return result.reshape(1, C, NB, BS**3)
-
-    def forward(weight):
-        return jnp.tile(weight.transpose(0, 2, 1), (1, 1, 4))
-
-    def backward(weight):
-        return jnp.tile(weight[::-1], (1, 1, 4))
-
-    weights = jnp.stack(
-        [
-            forward(weight_first),
-            forward(weight_second),
-            backward(weight_second),
-            backward(weight_first),
-        ]
-    )
-    scales = jnp.tile(jnp.stack([gain_first, bias_first, gain_second, bias_second]), (1, 4))
+    def flatten(array):
+        return array.reshape(C * NB, BS**3)
+
+    def row(vector):
+        return vector.reshape(1, C)
+
+    scale = 1.0 / float(tiles * regions * NB * BS**3) ** 0.5
+    piece = SUM_ROWS // tiles
     grid = pltpu.VMEM((GROUPS, TOTAL, LANES), F32)
     smem = pl.BlockSpec(memory_space=pltpu.SMEM)
     vmem = pl.BlockSpec(memory_space=pltpu.VMEM)
-    block_output, block_grad, wgrad = pl.pallas_call(
-        functools.partial(kernel, tiles_x),
+    block_output, block_grad, grad_first, grad_second = pl.pallas_call(
+        functools.partial(kernel, tiles, regions, scale),
         out_shape=(
-            jax.ShapeDtypeStruct((NB, BS * BS, BS * C), BF16),
-            jax.ShapeDtypeStruct((NB, BS * BS, BS * C), BF16),
-            jax.ShapeDtypeStruct((2, 27, C, LANES), F32),
+            jax.ShapeDtypeStruct((C * NB, BS**3), BF16),
+            jax.ShapeDtypeStruct((C * NB, BS**3), BF16),
+            jax.ShapeDtypeStruct((27, C, C), F32),
+            jax.ShapeDtypeStruct((27, C, C), F32),
         ),
-        in_specs=[smem, smem, vmem, vmem, vmem, vmem],
-        out_specs=(vmem, vmem, vmem),
+        in_specs=[smem] + [vmem] * 8,
+        out_specs=(vmem, vmem, vmem, vmem),
         scratch_shapes=[
             grid,
             grid,
@@ -457,30 +594,52 @@
             pltpu.VMEM((4, 9 * 256, 256), BF16),
             pltpu.VMEM((4, 5 * LANES, 256), BF16),
             pltpu.VMEM((GROUPS * LANES, OWN_ROWS), BF16),
-            pltpu.VMEM((NPOS + 1, BS * BS, BS * C), BF16),
+            pltpu.VMEM((NPOS + 1, BS * BS, BS * C), F32),
             pltpu.VMEM((2, 2, HALO * Y, 512), BF16),
             pltpu.VMEM((2, 2, HALO * X, 512), BF16),
             pltpu.VMEM((2, 4, 16, 512), BF16),
             pltpu.VMEM((2, 2, HALO * Y, 512), BF16),
             pltpu.VMEM((2, 2, HALO * X, 512), BF16),
             pltpu.VMEM((2, 4, 16, 512), BF16),
+            pltpu.VMEM((GROUPS, C * NB, LANES), F32),
+            pltpu.VMEM((NB, BS**3, LANES), F32),
+            pltpu.VMEM((NB + 1, BS * BS, BS * C), F32),
+            pltpu.VMEM((2, SUM_ROWS, LANES), F32),
+            pltpu.VMEM((2, tiles, piece, LANES), F32),
+            pltpu.VMEM((2, regions, piece, LANES), F32),
+            pltpu.VMEM((2, SUM_ROWS, LANES), F32),
             pltpu.SemaphoreType.DMA((2, 8)),
             pltpu.SemaphoreType.DMA((2, 8)),
+            pltpu.SemaphoreType.DMA((2, tiles)),
+            pltpu.SemaphoreType.DMA((2, tiles)),
+            pltpu.SemaphoreType.DMA((2, regions)),
+            pltpu.SemaphoreType.DMA((2, regions)),
+            pltpu.SemaphoreType.DMA((2, tiles)),
+            pltpu.SemaphoreType.DMA((2, tiles)),
         ],
         compiler_params=pltpu.CompilerParams(
             collective_id=0, has_side_effects=True, vmem_limit_bytes=60 * 1024 * 1024
         ),
-    )(slot_of, slot_pos, to_rows(features, EMPTY), to_rows(cotangent, 0.0), weights, scales)
-    local = wgrad[:, :, :, :C] * (1.0 / jnp.sqrt(jnp.float32(voxels)))
-    summed = lax.psum(local, ("tile", "rep"))
-    return from_rows(block_output), from_rows(block_grad), summed[0], summed[1]
+    )(
+        positions,
+        flatten(features),
+        flatten(cotangent),
+        weight_first,
+        weight_second,
+        row(gain_first),
+        row(bias_first),
+        row(gain_second),
+        row(bias_second),
+    )
+    shape = (1, C, NB, BS**3)
+    return block_output.reshape(shape), block_grad.reshape(shape), grad_first, grad_second
 
 
 def solution(mesh):
     split = P("rep", None, "tile", None)
     tiles, regions = mesh.shape["tile"], mesh.shape["rep"]
     return jax.shard_map(
-        functools.partial(per_device, tiles // TGY, tiles * regions * NB * BS**3),
+        functools.partial(per_device, tiles, regions),
         mesh=mesh,
         in_specs=(split, split, P("rep", "tile"), P(), P(), P(), P(), P(), P()),
         out_specs=(split, split, P(), P()),

time: 204 us -> 51.8 us (0.25)
  waiting for transfers between devices: 125 us -> 0 us
  local copies, waits for them, and re-layouts: 20 us -> 4.38 us
  between operations: 14.2 us -> 0.66 us
  Pallas kernels: 40 us -> 46.6 us
  other arithmetic: 3.94 us -> 0 us
    psum x1 -> x0, waiting for transfers between devices: 125 us -> none  [per_device(): summed = lax.psum(local, ('tile', 'rep'))]
    pallas_call x1, Pallas kernels: 40 us -> 46.6 us  [per_device(): pl.pallas_call(functools.partial(kernel, tiles, regions, scale), out_shap...]
    another operation x10 -> x0, local copies, waits for them, and re-layouts: 3.95 us -> none  [the longest x4 1.64 us: backward(): return jnp.tile(weight[::-1], (1, 1, 4))]
    unnamed x26 -> x10, local copies, waits for them, and re-layouts: 7.76 us -> 4.38 us
    transpose x6 -> x0, local copies, waits for them, and re-layouts: 2.73 us -> none  [the longest x2 1.28 us: to_rows(): blocks = compact[0].reshape(C, NB, BS * BS, BS).transpose(1, 2, 3, 0)]
    mul x1 -> x0, other arithmetic: 2.19 us -> none  [per_device(): local = wgrad[:, :, :, :C] * (1.0 / jnp.sqrt(jnp.float32(voxels)))]
    squeeze x1 -> x0, local copies, waits for them, and re-layouts: 2.11 us -> none  [per_device(): summed[1]]
  transfers between devices with their start and end apart: 1 -> 0, of which waited for: 1 -> 0; matrix products, arithmetic and copies ran while one was open for 2% -> 0% of each run, Pallas kernels for 0% -> 0%
where the time goes in v1:
time: 51.8 us; the launch traced here: 51.6 us
  Pallas kernels  46.6 us (90%)
  local copies, waits for them, and re-layouts  4.38 us (8%)
  between operations  0.66 us (1%)
    pallas_call x1, Pallas kernels, per_device(): pl.pallas_call(functools.partial(kernel, tiles, regions, scale), out_shap...  46.6 us
    unnamed x10, local copies, waits for them, and re-layouts  4.38 us

profile of v1, /device:TPU:0, one launch (start us, length us, event | category | flops | bytes accessed | tf_op | source)
XLA Modules:
  0.0 51.6 jit_solution(13448166636752891465)
XLA Ops:
  0.6 46.6 %shard_map.120 = (bf16[256,512]{1,0:T(8,128)(2,1)}, bf16[256,512]{1,0:T(8,128)(2,1)}, f32[27,32,32]{2,1,0:T(8,128)}, f32[27,32,32]{2,1,0:T(8,128)}) custom-call(s32[1,8]{1,0:T(1,128)} %positions.1, bf16[256,512]{1,0:T(8,128)(2,1)} %bitcast.8, bf16[256,512]{1,0:T(8,128)(2,1)} %bitcast.9, bf16[27,32,32]{2,1,0:T(8,128)(2,1)} %weight_first.1, ...), custom_call_target="tpu_custom_call" | custom-call | tf_op jit(solution)/shard_map/pallas_call | solution.py:570
  47.2 0.0 copy-start.2
  47.2 0.0 copy-start.1
  47.2 1.7 %copy.17 = bf16[1,32,8,512]{3,2,1,0:T(8,128)(2,1)} copy(bf16[1,32,8,512]{3,2,1,0:T(8,128)(2,1)} %bitcast.11) | data formatting | bytes 524288
  49.0 0.0 copy-done.2
  49.0 0.7 %copy.18 = bf16[1,32,8,512]{3,2,1,0:T(8,128)(2,1)} copy(bf16[1,32,8,512]{3,2,1,0:T(8,128)(2,1)S(1)} %bitcast.10) | data formatting | bytes 524288
  49.7 0.0 copy-done.1
  49.7 0.0 copy-start
  49.7 0.8 %copy.19 = f32[27,32,32]{2,1,0:T(8,128)} copy(f32[27,32,32]{2,1,0:T(8,128)S(1)} %copy-done.1) | data formatting | bytes 221184
  50.4 0.4 copy-done
  50.9 0.8 %copy.20 = f32[27,32,32]{2,1,0:T(8,128)} copy(f32[27,32,32]{2,1,0:T(8,128)S(1)} %copy-done) | data formatting | bytes 221184
Async XLA Ops:
  47.2 1.8 %copy-start.2 = (bf16[256,512]{1,0:T(8,128)(2,1)S(1)}, bf16[256,512]{1,0:T(8,128)(2,1)}, u32[]{:S(2)}) copy-start(bf16[256,512]{1,0:T(8,128)(2,1)} %get-tuple-element.9) | copy-start | bytes 786436
  47.2 2.5 %copy-start.1 = (f32[27,32,32]{2,1,0:T(8,128)S(1)}, f32[27,32,32]{2,1,0:T(8,128)}, u32[]{:S(2)}) copy-start(f32[27,32,32]{2,1,0:T(8,128)} %get-tuple-element.18) | copy-start | bytes 331780
  49.7 1.2 %copy-start = (f32[27,32,32]{2,1,0:T(8,128)S(1)}, f32[27,32,32]{2,1,0:T(8,128)}, u32[]{:S(2)}) copy-start(f32[27,32,32]{2,1,0:T(8,128)} %get-tuple-element.19) | copy-start | bytes 331780

commit v2 on v1

--- a/solution.py
+++ b/solution.py
@@ -43,6 +43,10 @@
     return HALO + extent if way < 0 else 0
 
 
+def sigmoid(values):
+    return 0.5 + 0.5 * jnp.tanh(0.5 * values)
+
+
 def kernel(
     tiles,
     regions,
@@ -62,7 +66,7 @@
     wgrad_second,
     raw,
     field,
-    pre_one,
+    slope_one,
     hidden,
     cot,
     d_two,
@@ -432,8 +436,8 @@
         lax.fori_loop(0, 2, step, 0)
 
     def weight_gradient(taps, offset, which):
-        def step(t, carry):
-            lanes = pl.ds(pl.multiple_of(t * 256, 256), 256)
+        def step(x_tap, carry):
+            lanes = pl.ds(pl.multiple_of(x_tap * 768, 256), 768)
             products = [
                 jnp.dot(
                     turned[half * 224 : half * 224 + 288, :],
@@ -442,24 +446,24 @@
                 )
                 for half in range(2)
             ]
-            for dz in range(-1, 2):
-                total = jnp.zeros((C, LANES), F32)
-                for half in range(2):
-                    for b in range(8):
-                        a = b + half - dz
-                        if 0 <= a <= 8:
-                            part = products[half][
-                                a * C : (a + 1) * C, b // 4 * LANES : (b // 4 + 1) * LANES
-                            ]
-                            total = total + jnp.where(lane_group == b % 4, part, 0.0)
-                total = total + pltpu.roll(total, 64, 1)
-                total = total + pltpu.roll(total, 32, 1)
-                q = t * 3 + (dz + 1)
-                rows = pl.ds(pl.multiple_of(lax.div(q, 4) * C, C), C)
-                sums[which, rows, :] += jnp.where(lane_group == lax.rem(q, 4), total, 0.0)
+            for y_tap in range(3):
+                for dz in range(-1, 2):
+                    total = jnp.zeros((C, LANES), F32)
+                    for half in range(2):
+                        for b in range(8):
+                            a = b + half - dz
+                            if 0 <= a <= 8:
+                                begin = y_tap * 256 + b // 4 * LANES
+                                part = products[half][a * C : (a + 1) * C, begin : begin + LANES]
+                                total = total + jnp.where(lane_group == b % 4, part, 0.0)
+                    total = total + pltpu.roll(total, 64, 1)
+                    total = total + pltpu.roll(total, 32, 1)
+                    q = x_tap * 9 + (y_tap * 3 + dz + 1)
+                    rows = pl.ds(pl.multiple_of(lax.div(q, 4) * C, C), C)
+                    sums[which, rows, :] += jnp.where(lane_group == lax.rem(q, 4), total, 0.0)
             return carry
 
-        lax.fori_loop(0, 9, step, 0)
+        lax.fori_loop(0, 3, step, 0)
 
     def wide(ref):
         return jnp.concatenate([ref[...]] * 4, axis=1)
@@ -478,10 +482,12 @@
 
     def after_first(g, rows, value):
         pre = value * gain_one + bias_one
-        pre_one[g, rows, :] = pre
-        act = pre / (1.0 + jnp.exp(-pre))
-        act = jnp.where(raw[g, rows, :] < 512.0, act, 0.0)
-        hidden[g, rows, :] = act.astype(BF16).astype(F32)
+        active = raw[g, rows, :] < 512.0
+        s = sigmoid(pre)
+        act = pre * s
+        slope = (s + act * (1.0 - s)) * gain_one
+        slope_one[g, rows, :] = jnp.where(active, slope, 0.0)
+        hidden[g, rows, :] = jnp.where(active, act, 0.0).astype(BF16).astype(F32)
 
     convolve(taps_one, 0, WIDE_START, WIDE_ROWS, after_first)
 
@@ -489,9 +495,10 @@
 
     def after_second(g, rows, value):
         pre = value * gain_two + bias_two + field[g, rows, :]
-        s = 1.0 / (1.0 + jnp.exp(-pre))
-        hidden[g, rows, :] = pre * s
-        d = cot[g, rows, :] * (s + pre * s * (1.0 - s))
+        s = sigmoid(pre)
+        act = pre * s
+        hidden[g, rows, :] = act
+        d = cot[g, rows, :] * (s + act * (1.0 - s))
         d_two[g, rows, :] = d
         e_two[g, rows, :] = (d * gain_two).astype(BF16).astype(F32)
 
@@ -511,11 +518,7 @@
     gather_taps(e_two, taps_back, WIDE_START, WIDE_ROWS)
 
     def after_third(g, rows, value):
-        pre = pre_one[g, rows, :]
-        s = 1.0 / (1.0 + jnp.exp(-pre))
-        e = value * (s + pre * s * (1.0 - s)) * gain_one
-        e = jnp.where(raw[g, rows, :] < 512.0, e, 0.0)
-        e_one[g, rows, :] = e.astype(BF16).astype(F32)
+        e_one[g, rows, :] = (value * slope_one[g, rows, :]).astype(BF16).astype(F32)
 
     convolve(taps_back, 2, WIDE_START, WIDE_ROWS, after_third)
 

time: 51.8 us -> 47.6 us (0.919)
  Pallas kernels: 46.6 us -> 42.4 us
    pallas_call x1, Pallas kernels: 46.6 us -> 42.4 us  [per_device(): pl.pallas_call(functools.partial(kernel, tiles, regions, scale), out_shap...]
where the time goes in v2:
time: 47.6 us; the launch traced here: 47.4 us
  Pallas kernels  42.4 us (89%)
  local copies, waits for them, and re-layouts  4.38 us (9%)
  between operations  0.66 us (1%)
    pallas_call x1, Pallas kernels, per_device(): pl.pallas_call(functools.partial(kernel, tiles, regions, scale), out_shap...  42.4 us
    unnamed x10, local copies, waits for them, and re-layouts  4.38 us

profile of v2, /device:TPU:0, one launch (start us, length us, event | category | flops | bytes accessed | tf_op | source)
XLA Modules:
  0.0 47.4 jit_solution(2767470241099049618)
XLA Ops:
  0.6 42.4 %shard_map.120 = (bf16[256,512]{1,0:T(8,128)(2,1)}, bf16[256,512]{1,0:T(8,128)(2,1)}, f32[27,32,32]{2,1,0:T(8,128)}, f32[27,32,32]{2,1,0:T(8,128)}) custom-call(s32[1,8]{1,0:T(1,128)} %positions.1, bf16[256,512]{1,0:T(8,128)(2,1)} %bitcast.8, bf16[256,512]{1,0:T(8,128)(2,1)} %bitcast.9, bf16[27,32,32]{2,1,0:T(8,128)(2,1)} %weight_first.1, ...), custom_call_target="tpu_custom_call" | custom-call | tf_op jit(solution)/shard_map/pallas_call | solution.py:573
  43.0 0.0 copy-start.2
  43.0 0.0 copy-start.1
  43.0 1.7 %copy.17 = bf16[1,32,8,512]{3,2,1,0:T(8,128)(2,1)} copy(bf16[1,32,8,512]{3,2,1,0:T(8,128)(2,1)} %bitcast.11) | data formatting | bytes 524288
  44.8 0.0 copy-done.2
  44.8 0.7 %copy.18 = bf16[1,32,8,512]{3,2,1,0:T(8,128)(2,1)} copy(bf16[1,32,8,512]{3,2,1,0:T(8,128)(2,1)S(1)} %bitcast.10) | data formatting | bytes 524288
  45.5 0.0 copy-done.1
  45.5 0.0 copy-start
  45.5 0.8 %copy.19 = f32[27,32,32]{2,1,0:T(8,128)} copy(f32[27,32,32]{2,1,0:T(8,128)S(1)} %copy-done.1) | data formatting | bytes 221184
  46.3 0.4 copy-done
  46.7 0.8 %copy.20 = f32[27,32,32]{2,1,0:T(8,128)} copy(f32[27,32,32]{2,1,0:T(8,128)S(1)} %copy-done) | data formatting | bytes 221184
Async XLA Ops:
  43.0 1.8 %copy-start.2 = (bf16[256,512]{1,0:T(8,128)(2,1)S(1)}, bf16[256,512]{1,0:T(8,128)(2,1)}, u32[]{:S(2)}) copy-start(bf16[256,512]{1,0:T(8,128)(2,1)} %get-tuple-element.9) | copy-start | bytes 786436
  43.0 2.5 %copy-start.1 = (f32[27,32,32]{2,1,0:T(8,128)S(1)}, f32[27,32,32]{2,1,0:T(8,128)}, u32[]{:S(2)}) copy-start(f32[27,32,32]{2,1,0:T(8,128)} %get-tuple-element.18) | copy-start | bytes 331780
  45.5 1.2 %copy-start = (f32[27,32,32]{2,1,0:T(8,128)S(1)}, f32[27,32,32]{2,1,0:T(8,128)}, u32[]{:S(2)}) copy-start(f32[27,32,32]{2,1,0:T(8,128)} %get-tuple-element.19) | copy-start | bytes 331780

commit v3 on v2

--- a/solution.py
+++ b/solution.py
@@ -433,7 +433,7 @@
             finish_group(3, there, high[:, LANES:])
             return carry
 
-        lax.fori_loop(0, 2, step, 0)
+        lax.fori_loop(0, 2, step, 0, unroll=True)
 
     def weight_gradient(taps, offset, which):
         def step(x_tap, carry):
@@ -463,7 +463,7 @@
                     sums[which, rows, :] += jnp.where(lane_group == lax.rem(q, 4), total, 0.0)
             return carry
 
-        lax.fori_loop(0, 3, step, 0)
+        lax.fori_loop(0, 3, step, 0, unroll=True)
 
     def wide(ref):
         return jnp.concatenate([ref[...]] * 4, axis=1)

time: 47.6 us -> 42.2 us (0.89)
  Pallas kernels: 42.4 us -> 36.9 us
    pallas_call x1, Pallas kernels: 42.4 us -> 36.9 us  [per_device(): pl.pallas_call(functools.partial(kernel, tiles, regions, scale), out_shap...]
where the time goes in v3:
time: 42.2 us; the launch traced here: 42 us
  Pallas kernels  36.9 us (87%)
  local copies, waits for them, and re-layouts  4.38 us (10%)
  between operations  0.66 us (2%)
    pallas_call x1, Pallas kernels, per_device(): pl.pallas_call(functools.partial(kernel, tiles, regions, scale), out_shap...  36.9 us
    unnamed x10, local copies, waits for them, and re-layouts  4.38 us

profile of v3, /device:TPU:0, one launch (start us, length us, event | category | flops | bytes accessed | tf_op | source)
XLA Modules:
  0.0 42.0 jit_solution(873161752679480542)
XLA Ops:
  0.6 36.9 %shard_map.120 = (bf16[256,512]{1,0:T(8,128)(2,1)}, bf16[256,512]{1,0:T(8,128)(2,1)}, f32[27,32,32]{2,1,0:T(8,128)}, f32[27,32,32]{2,1,0:T(8,128)}) custom-call(s32[1,8]{1,0:T(1,128)} %positions.1, bf16[256,512]{1,0:T(8,128)(2,1)} %bitcast.8, bf16[256,512]{1,0:T(8,128)(2,1)} %bitcast.9, bf16[27,32,32]{2,1,0:T(8,128)(2,1)} %weight_first.1, ...), custom_call_target="tpu_custom_call" | custom-call | tf_op jit(solution)/shard_map/pallas_call | solution.py:573
  37.6 0.0 copy-start.2
  37.6 0.0 copy-start.1
  37.6 1.7 %copy.17 = bf16[1,32,8,512]{3,2,1,0:T(8,128)(2,1)} copy(bf16[1,32,8,512]{3,2,1,0:T(8,128)(2,1)} %bitcast.11) | data formatting | bytes 524288
  39.3 0.0 copy-done.2
  39.3 0.7 %copy.18 = bf16[1,32,8,512]{3,2,1,0:T(8,128)(2,1)} copy(bf16[1,32,8,512]{3,2,1,0:T(8,128)(2,1)S(1)} %bitcast.10) | data formatting | bytes 524288
  40.0 0.0 copy-done.1
  40.1 0.0 copy-start
  40.1 0.8 %copy.19 = f32[27,32,32]{2,1,0:T(8,128)} copy(f32[27,32,32]{2,1,0:T(8,128)S(1)} %copy-done.1) | data formatting | bytes 221184
  40.8 0.4 copy-done
  41.2 0.8 %copy.20 = f32[27,32,32]{2,1,0:T(8,128)} copy(f32[27,32,32]{2,1,0:T(8,128)S(1)} %copy-done) | data formatting | bytes 221184
Async XLA Ops:
  37.6 1.8 %copy-start.2 = (bf16[256,512]{1,0:T(8,128)(2,1)S(1)}, bf16[256,512]{1,0:T(8,128)(2,1)}, u32[]{:S(2)}) copy-start(bf16[256,512]{1,0:T(8,128)(2,1)} %get-tuple-element.9) | copy-start | bytes 786436
  37.6 2.5 %copy-start.1 = (f32[27,32,32]{2,1,0:T(8,128)S(1)}, f32[27,32,32]{2,1,0:T(8,128)}, u32[]{:S(2)}) copy-start(f32[27,32,32]{2,1,0:T(8,128)} %get-tuple-element.18) | copy-start | bytes 331780
  40.1 1.2 %copy-start = (f32[27,32,32]{2,1,0:T(8,128)S(1)}, f32[27,32,32]{2,1,0:T(8,128)}, u32[]{:S(2)}) copy-start(f32[27,32,32]{2,1,0:T(8,128)} %get-tuple-element.19) | copy-start | bytes 331780
